TPU v7x, 32 devices: a whole 2x2x4 slice. The times are simulated.
32 devices in a mesh: space: 8 (over z, y), mode: 4 (over x, core).
Axes of the slice: x: 2, y: 2, z: 4, core: 2. Of those that a mesh axis runs over, the one named last changes fastest.
Arguments:
- iterate: float32 [84, 16, 6144], P('mode', None, 'space'), may hold values from -6 to 6
- forcing: float32 [84, 16, 6144], P('mode', None, 'space'), may hold values from -6 to 6
- tiles: bfloat16 [3, 32, 3, 36864], P(None, 'space'), may hold values from -0.25 to 0.25
- inverse_blocks: bfloat16 [32, 36864], P('space'), may hold values from -0.4375 to 0.4375
- columns: int32 [32, 3], P('space'), may hold values from 0 to 7, as said below
- coupling: float32 [3, 84, 84], replicated, may hold values from -0.7 to 1.5, as said below
Outputs:
- updated: float32 [84, 16, 6144], P('mode', None, 'space')
- residual: float32 [84, 16, 6144], P('mode', None, 'space')
Inputs may be any that keep to these rules, and one draw needn't show every extreme that they name: For row block j at position q = j mod 4 of its device: columns[j, 0] = 2 + q; columns[j, 1] = 2 + q - 1 or 2 + q - 2; columns[j, 2] = 2 + q + 1 or 2 + q + 2. At q = 0 slot 1 is 2 + q - 2, at q = 3 slot 2 is 2 + q + 2. `coupling`: each matrix is symmetric; the first has ones added on its diagonal.
All inputs are finite; a program needn't handle non-finite values.
Results may differ from a plain program's by a relative error of at most 0.0033.
Values may be sent and summed in bfloat16 or wider, within the bound.
A program may use at most 64 MiB of HBM per device.

v0:
```python
import jax
import jax.numpy as jnp
from jax import lax
from jax.sharding import PartitionSpec as P

H = 2


RELAXATION = 0.7


def padded(x, sides, width):
    for axis, dim in sides:
        devices, length = (lax.axis_size(axis), x.shape[dim])
        up = [(i, (i + 1) % devices) for i in range(devices)]
        down = [(j, i) for i, j in up]
        last = lax.slice_in_dim(x, length - width, length, axis=dim)
        initial = lax.slice_in_dim(x, 0, width, axis=dim)
        before = lax.ppermute(last, axis, up)
        after = lax.ppermute(initial, axis, down)
        x = jnp.concatenate([before, x, after], axis=dim)
    return x


def stiffness(extended, tile_rows, column_rows):
    block_size = extended.shape[-1]
    picked = jnp.take(extended, column_rows, axis=2)
    shaped = tile_rows.reshape(
        tile_rows.shape[0], tile_rows.shape[1], tile_rows.shape[2], block_size, block_size
    )
    return jnp.einsum("krsim,plrsm->kplri", shaped, picked, preferred_element_type=jnp.float32)


def body(iterate, forcing, tiles, inverse_blocks, columns, coupling):
    modes_here, loads, dofs_here = iterate.shape
    terms, block_count = (tiles.shape[0], tiles.shape[1])
    block_size = dofs_here // block_count
    rounded = iterate.astype(jnp.bfloat16).reshape(modes_here, loads, block_count, block_size)
    extended = padded(rounded, (("space", 2),), H)
    products = stiffness(extended, tiles, columns).astype(jnp.bfloat16)
    mixture = jnp.einsum(
        "kab,kblqn->alqn",
        coupling,
        lax.all_to_all(products, "mode", split_axis=3, concat_axis=1, tiled=True).astype(
            jnp.float32
        ),
        precision=lax.Precision.HIGHEST,
    )
    applied = lax.all_to_all(mixture, "mode", split_axis=0, concat_axis=2, tiled=True)
    applied = applied.reshape(modes_here, loads, dofs_here)
    residual = forcing - applied
    rounded_res = residual.astype(jnp.bfloat16).reshape(modes_here, loads, block_count, block_size)
    inverse = inverse_blocks.reshape(block_count, block_size, block_size)
    update = jnp.einsum("jim,pljm->plji", inverse, rounded_res, preferred_element_type=jnp.float32)
    updated = iterate + RELAXATION * update.reshape(modes_here, loads, dofs_here)
    return (updated, residual)


def solution(mesh):
    return jax.shard_map(
        body,
        mesh=mesh,
        in_specs=(
            P("mode", None, "space"),
            P("mode", None, "space"),
            P(None, "space", None, None),
            P("space", None),
            P("space", None),
            P(),
        ),
        out_specs=(P("mode", None, "space"), P("mode", None, "space")),
        check_vma=False,
    )
```

profile of v0, /device:TPU:0, one launch (start us, length us, event | category | flops | bytes accessed | tf_op | source)
XLA Modules:
  0.0 92.3 jit_solution(9699311394630244331)
XLA Ops:
  0.6 0.0 copy-start
  0.6 1.3 %convert_element_type.13 = bf16[21,16,768]{2,1,0:T(8,128)(2,1)S(1)} convert(f32[21,16,768]{2,1,0:T(8,128)} %param.6) | non-fusion elementwise | flops 258048 | bytes 1548288 | tf_op jit(solution)/shard_map/convert_element_type | solution.py:38
  2.0 0.0 copy-start.2
  2.0 0.6 reshape.33
  2.6 0.1 copy.28
  2.7 3.0 %collective-permute-start = (bf16[21,16,2,192]{3,1,2,0:T(8,128)(2,1)S(1)}, bf16[21,16,2,192]{3,1,2,0:T(8,128)(2,1)S(1)}, u32[]{:S(2)}, u32[]{:S(2)}) collective-permute-start(bf16[21,16,2,192]{3,1,2,0:T(8,128)(2,1)S(1)} %get-tuple-element.4), channel_id=1, source_target_pairs={{0,4},{4,8},{8,12},{12,16},{16,20},{20,24},{24,28},{28,0},{1,5},{5... | collective-permute-start | bytes 774152 | tf_op jit(solution)/shard_map/ppermute | solution.py:19
  5.8 3.1 %collective-permute-start.1 = (bf16[21,16,2,192]{3,1,2,0:T(8,128)(2,1)S(1)}, bf16[21,16,2,192]{3,1,2,0:T(8,128)(2,1)S(1)}, u32[]{:S(2)}, u32[]{:S(2)}) collective-permute-start(bf16[21,16,2,192]{3,1,2,0:T(8,128)(2,1)S(1)} %get-tuple-element.5), channel_id=1, source_target_pairs={{4,0},{8,4},{12,8},{16,12},{20,16},{24,20},{28,24},{0,28},{5,1},{9... | collective-permute-start | bytes 774152 | tf_op jit(solution)/shard_map/ppermute | solution.py:20
  8.9 0.0 copy-done.2
  8.9 0.1 reshape.41
  9.0 6.5 %reshape.34 = bf16[3,4,3,192,192]{4,3,1,2,0:T(8,128)(2,1)} reshape(bf16[3,4,3,36864]{3,1,2,0:T(4,128)(2,1)} %param.8) | data formatting | bytes 5308416 | tf_op jit(solution)/shard_map/reshape | solution.py:28
  15.4 5.0 %collective-permute-done = bf16[21,16,2,192]{3,1,2,0:T(8,128)(2,1)S(1)} collective-permute-done((bf16[21,16,2,192]{3,1,2,0:T(8,128)(2,1)S(1)}, bf16[21,16,2,192]{3,1,2,0:T(8,128)(2,1)S(1)}, u32[]{:S(2)}, u32[]{:S(2)}) %collective-permute-start) | collective-permute-done | bytes 258080 | tf_op jit(solution)/shard_map/ppermute | solution.py:19
  20.5 2.2 %collective-permute-done.1 = bf16[21,16,2,192]{3,1,2,0:T(8,128)(2,1)S(1)} collective-permute-done((bf16[21,16,2,192]{3,1,2,0:T(8,128)(2,1)S(1)}, bf16[21,16,2,192]{3,1,2,0:T(8,128)(2,1)S(1)}, u32[]{:S(2)}, u32[]{:S(2)}) %collective-permute-start.1) | collective-permute-done | bytes 258080 | tf_op jit(solution)/shard_map/ppermute | solution.py:20
  22.7 0.3 pad_maximum_fusion
  22.9 2.1 %gather_fusion = bf16[12,21,16,192]{3,2,1,0:T(8,128)(2,1)} fusion(bf16[21,16,8,192]{3,1,2,0:T(8,128)(2,1)S(1)} %pad_maximum_fusion, s32[1024]{0:T(1024)S(1)} %pad_clamp_fusion), kind=kCustom, calls=%fused_computation | custom fusion | bytes 3096624 | tf_op jit(solution)/shard_map/jit(_take)/gather | solution.py:27
  25.0 4.4 %fusion.4 = bf16[3,21,16,4,192]{4,2,0,1,3:T(8,128)(2,1)S(1)} fusion(bf16[3,4,3,192,192]{4,3,1,2,0:T(8,128)(2,1)} %reshape.34, bf16[4,3,21,16,192]{4,3,2,1,0:T(8,128)(2,1)} %bitcast.47, pred[4,3]{1,0:T(4,128)(4,1)S(1)} %compare_and_fusion), kind=kOutput, calls=%fused_computation.6 | convolution fusion | flops 893362176 | bytes 5750796 | tf_op jit(solution)/shard_map/krsim,plrsm->kplri/dot_general | solution.py:31
  29.5 27.9 %all_to_all.30 = bf16[3,21,16,4,192]{4,2,0,1,3:T(8,128)(2,1)S(1)} all-to-all(bf16[3,21,16,4,192]{4,2,0,1,3:T(8,128)(2,1)S(1)} %fusion.4), channel_id=1, replica_groups=mesh['space'=8,'mode'=4] {'mode'}, dimensions={3} | all-to-all | bytes 3096576 | tf_op jit(solution)/shard_map/all_to_all | solution.py:44
  57.4 0.0 copy-done
  57.4 2.1 %fusion.10 = f32[84,16,1,192]{3,0,1,2:T(8,128)S(1)} fusion(bf16[3,84,16,192]{3,2,0,1:T(8,128)(2,1)S(1)} %bitcast.45, f32[3,84,84]{2,1,0:T(8,128)S(1)} %copy-done), kind=kOutput, calls=%fused_computation.9 | convolution fusion | flops 780337152 | bytes 2665152 | tf_op jit(solution)/shard_map/kab,kblqn->alqn/dot_general | solution.py:41
  59.5 1.5 %copy.34 = f32[84,16,1,192]{3,1,2,0:T(8,128)} copy(f32[84,16,1,192]{3,0,1,2:T(8,128)S(1)} %fusion.10) | data formatting | bytes 2064384 | tf_op jit(solution)/shard_map/kab,kblqn->alqn/dot_general | solution.py:41
  61.0 0.0 copy-start.1
  61.0 3.9 %all-to-all-start.1 = ((f32[84,16,1,192]{3,1,2,0:T(8,128)}), f32[84,16,1,192]{3,1,2,0:T(8,128)S(1)}, u32[]{:S(2)}, u32[]{:S(2)}) async-start(f32[84,16,1,192]{3,1,2,0:T(8,128)} %copy.34), calls=%async_computation.1 | async-start | bytes 2752512 | tf_op jit(solution)/shard_map/all_to_all | solution.py:49
  64.9 0.0 copy-done.1
  64.9 0.4 reshape.54
  65.3 17.3 %all-to-all-done.1 = f32[84,16,1,192]{3,1,2,0:T(8,128)S(1)} async-done(((f32[84,16,1,192]{3,1,2,0:T(8,128)}), f32[84,16,1,192]{3,1,2,0:T(8,128)S(1)}, u32[]{:S(2)}, u32[]{:S(2)}) %all-to-all-start.1) | async-done | bytes 1032224 | tf_op jit(solution)/shard_map/all_to_all | solution.py:49
  82.6 1.0 %copy.35 = f32[21,16,4,1,192]{4,2,1,0,3:T(4,128)S(1)} copy(f32[21,16,4,1,192]{4,1,0,2,3:T(8,128)S(1)} %bitcast.46) | data formatting | bytes 2064384 | tf_op jit(solution)/shard_map/all_to_all | solution.py:49
  83.7 0.9 reshape.36
  84.6 2.4 %fusion.17 = (bf16[21,16,768]{2,1,0:T(8,128)(2,1)S(1)}, f32[21,16,768]{2,1,0:T(8,128)}) fusion(f32[21,16,768]{2,1,0:T(8,128)} %param.7, f32[21,16,768]{2,1,0:T(8,128)S(1)} %reshape.36), kind=kLoop, calls=%fused_computation.19 | loop fusion | flops 516096 | bytes 3612672 | tf_op jit(solution)/shard_map/convert_element_type | solution.py:52
  87.0 0.6 reshape.37
  87.6 0.4 fusion.13
  88.0 1.0 %copy.37 = f32[21,16,4,192]{3,2,1,0:T(4,128)S(1)} copy(f32[21,16,4,192]{3,1,0,2:T(8,128)S(1)} %fusion.13) | data formatting | bytes 2064384 | tf_op jit(solution)/shard_map/mul | solution.py:55
  89.0 0.9 mul.15
  90.0 2.4 %add.8 = f32[21,16,768]{2,1,0:T(8,128)} add(f32[21,16,768]{2,1,0:T(8,128)} %param.6, f32[21,16,768]{2,1,0:T(8,128)S(1)} %mul.15) | non-fusion elementwise | flops 258048 | bytes 3096576 | tf_op jit(solution)/shard_map/add | solution.py:55
  (4 shorter events, 0.1 us)
Async XLA Ops:
  0.6 56.7 %copy-start = (f32[3,84,84]{2,1,0:T(8,128)S(1)}, f32[3,84,84]{2,1,0:T(8,128)}, u32[]{:S(2)}) copy-start(f32[3,84,84]{2,1,0:T(8,128)} %param.11) | copy-start | bytes 254020
  2.0 6.9 %copy-start.2 = (s32[4,3]{1,0:T(4,128)S(1)}, s32[4,3]{1,0:T(4,128)}, u32[]{:S(2)}) copy-start(s32[4,3]{1,0:T(4,128)} %param.10) | copy-start | bytes 148
  2.7 17.7 %collective-permute-start = (bf16[21,16,2,192]{3,1,2,0:T(8,128)(2,1)S(1)}, bf16[21,16,2,192]{3,1,2,0:T(8,128)(2,1)S(1)}, u32[]{:S(2)}, u32[]{:S(2)}) collective-permute-start(bf16[21,16,2,192]{3,1,2,0:T(8,128)(2,1)S(1)} %get-tuple-element.4), channel_id=1, source_target_pairs={{0,4},{4,8},{8,12},{12,16},{16,20},{20,24},{24,28},{28,0},{1,5},{5... | collective-permute-start | bytes 774152 | tf_op jit(solution)/shard_map/ppermute | solution.py:19
  5.8 16.9 %collective-permute-start.1 = (bf16[21,16,2,192]{3,1,2,0:T(8,128)(2,1)S(1)}, bf16[21,16,2,192]{3,1,2,0:T(8,128)(2,1)S(1)}, u32[]{:S(2)}, u32[]{:S(2)}) collective-permute-start(bf16[21,16,2,192]{3,1,2,0:T(8,128)(2,1)S(1)} %get-tuple-element.5), channel_id=1, source_target_pairs={{4,0},{8,4},{12,8},{16,12},{20,16},{24,20},{28,24},{0,28},{5,1},{9... | collective-permute-start | bytes 774152 | tf_op jit(solution)/shard_map/ppermute | solution.py:20
  61.0 3.9 %copy-start.1 = (bf16[4,36864]{1,0:T(4,128)(2,1)S(1)}, bf16[4,36864]{1,0:T(4,128)(2,1)}, u32[]{:S(2)}) copy-start(bf16[4,36864]{1,0:T(4,128)(2,1)} %param.9) | copy-start | bytes 884740
  61.0 21.6 %all-to-all-start.1 = ((f32[84,16,1,192]{3,1,2,0:T(8,128)}), f32[84,16,1,192]{3,1,2,0:T(8,128)S(1)}, u32[]{:S(2)}, u32[]{:S(2)}) async-start(f32[84,16,1,192]{3,1,2,0:T(8,128)} %copy.34), calls=%async_computation.1 | async-start | bytes 2752512 | tf_op jit(solution)/shard_map/all_to_all | solution.py:49
where the time goes:
time: 92.8 us; the launch traced here: 92.3 us
  blocking collectives  27.9 us (30%)
  waiting for transfers between devices  24.5 us (26%)
  local copies, waits for them, and re-layouts  15.9 us (17%)
  starting transfers between devices  9.98 us (11%)
  matrix products  6.89 us (7%)
  other arithmetic  6.38 us (7%)
    all_to_all x1, blocking collectives, body(): lax.all_to_all(products, 'mode', split_axis=3, concat_axis=1, tiled=True)  27.9 us
    all_to_all x1, waiting for transfers between devices, body(): lax.all_to_all(mixture, 'mode', split_axis=0, concat_axis=2, tiled=True)  17.3 us
    reshape x1, local copies, waits for them, and re-layouts, stiffness(): tile_rows.reshape(tile_rows.shape[0], tile_rows.shape[1], tile_rows.shape...  6.46 us
    ppermute x1, waiting for transfers between devices, padded(): before = lax.ppermute(last, axis, up)  5.02 us
    dot_general x1, matrix products, stiffness(): jnp.einsum('krsim,plrsm->kplri', shaped, picked, preferred_element_type=j...  4.43 us
    all_to_all x1, starting transfers between devices, body(): lax.all_to_all(mixture, 'mode', split_axis=0, concat_axis=2, tiled=True)  3.86 us
    ppermute x1, starting transfers between devices, padded(): after = lax.ppermute(initial, axis, down)  3.1 us
    ppermute x1, starting transfers between devices, padded(): before = lax.ppermute(last, axis, up)  3.02 us
  transfers between devices with their start and end apart: 3, of which 3 were waited for; matrix products, arithmetic and copies ran while one was open for 8% of the time, Pallas kernels for 0%

commit v1 on v0

v1 whole, which is shorter than its diff:
```python
import functools

import jax
import jax.numpy as jnp
from jax import lax
from jax.experimental import pallas as pl
from jax.experimental.pallas import tpu as pltpu
from jax.sharding import PartitionSpec as P

RELAXATION = 0.7
BF = jnp.bfloat16
F32 = jnp.float32
MESH = pl.DeviceIdType.MESH
ANY = pl.BlockSpec(memory_space=pl.ANY)


def nt(a, b):
    return lax.dot_general(a, b, (((1,), (1,)), ((), ())), preferred_element_type=F32)


def nn(a, b):
    return jnp.dot(a, b, preferred_element_type=F32)


def iota(shape, dim):
    return lax.broadcasted_iota(jnp.int32, shape, dim)


def kernel(
    cfg,
    cols_ref, it_ref, c_ref, fo_hbm, tiles_hbm, inv_hbm,
    upd_ref, res_ref,
    fo_ref, tiles_ref, inv_ref, xe, acc, prod, kron, own, a_out, a_in, b_out, b_in, c_out, c_in,
    lsem, hs, hr, as_, ar, bs, br, cs, cr,
):
    modes, loads, bsz, terms, seg = cfg
    rows = modes * loads
    half = 2 * bsz
    n_space = lax.axis_size("space")
    me_s = lax.axis_index("space")
    me = lax.axis_index("mode")
    right = lax.rem(me_s + 1, n_space)
    left = lax.rem(me_s + n_space - 1, n_space)
    near = me + 1 - 2 * lax.rem(me, 2)
    far = lax.rem(me + 2, 4)
    diag = lax.rem(near + 2, 4)
    to_right, to_left = (right, me), (left, me)
    to_near, to_far = (me_s, near), (me_s, far)

    loads_in = [
        pltpu.make_async_copy(tiles_hbm, tiles_ref, lsem.at[0]),
        pltpu.make_async_copy(fo_hbm, fo_ref, lsem.at[1]),
        pltpu.make_async_copy(inv_hbm, inv_ref, lsem.at[2]),
    ]
    for cp in loads_in:
        cp.start()

    barrier = pltpu.get_barrier_semaphore()
    for who in (to_right, to_left, to_near, to_far):
        pl.semaphore_signal(barrier, inc=1, device_id=who, device_id_type=MESH)
    for h in range(2):
        xe[1 + h] = it_ref[:, h * half : (h + 1) * half].astype(BF)
    pl.semaphore_wait(barrier, 4)

    def remote(src, dst, s, r, who):
        return pltpu.make_async_remote_copy(
            src_ref=src, dst_ref=dst, send_sem=s, recv_sem=r, device_id=who, device_id_type=MESH
        )

    halo = [
        remote(xe.at[2], xe.at[0], hs.at[0], hr.at[0], to_right),
        remote(xe.at[1], xe.at[3], hs.at[1], hr.at[1], to_left),
    ]
    for cp in halo:
        cp.start()

    total = c_ref.shape[1]
    col = iota((total, seg), 1)
    pick = (iota((total, seg), 0) == me * modes + col // loads) & (col < rows)
    pick = jnp.where(pick, 1.0, 0.0).astype(BF)
    spread = [nn(c_ref[k].astype(BF), pick).astype(BF) for k in range(terms)]
    same = (iota((rows, seg), 0) % loads) == (iota((rows, seg), 1) % loads)
    for n, dest in enumerate((diag, far, near, me)):
        e = iota((rows, total), 1) == dest * modes + iota((rows, total), 0) // loads
        e = jnp.where(e, 1.0, 0.0).astype(BF)
        for k in range(terms):
            kron[n, :, k * seg : (k + 1) * seg] = jnp.where(same, nn(e, spread[k]), 0.0).astype(BF)
    for h in range(2):
        for k in range(terms):
            prod[h, k * seg + rows : (k + 1) * seg, :] = jnp.zeros((seg - rows, half), BF)

    def block(q):
        p = q + 2
        return xe[p // 2, :, (p % 2) * bsz : (p % 2 + 1) * bsz]

    loads_in[0].wait()

    def early(q, s):
        near_, far_ = (q - 1, q - 2) if s == 1 else (q + 1, q + 2)
        return jnp.where(cols_ref[q, s] == near_ + 2, block(near_), block(far_))

    for q in range(4):
        s = 2 if q < 2 else 1
        a0, a1 = block(q), early(q, s)
        for k in range(terms):
            acc[k, q] = nt(a0, tiles_ref[k, 0, q]) + nt(a1, tiles_ref[k, s, q])

    for cp in halo:
        cp.wait()

    def late(h):
        for q in (2 * h, 2 * h + 1):
            s = 1 if q < 2 else 2
            if q == 0:
                x = block(-2)
            elif q == 3:
                x = block(5)
            else:
                x = early(q, s)
            for k in range(terms):
                y = acc[k, q] + nt(x, tiles_ref[k, s, q])
                prod[h, k * seg : k * seg + rows, (q % 2) * bsz : (q % 2 + 1) * bsz] = y.astype(BF)

    def mix(n, h):
        return nn(kron[n], prod[h])

    ca = [remote(a_out.at[h], a_in.at[h], as_.at[h], ar.at[h], to_near) for h in range(2)]
    cb = [remote(b_out.at[h], b_in.at[h], bs.at[h], br.at[h], to_far) for h in range(2)]
    cc = [remote(c_out.at[h], c_in.at[h], cs.at[h], cr.at[h], to_near) for h in range(2)]
    for h in range(2):
        late(h)
        a_out[h] = mix(0, h).astype(BF)
        ca[h].start()
        t = mix(1, h)
        ca[h].wait()
        b_out[h] = (t + a_in[h].astype(F32)).astype(BF)
        cb[h].start()
    for h in range(2):
        c_out[h] = mix(2, h).astype(BF)
        cc[h].start()
    loads_in[1].wait()
    loads_in[2].wait()
    for h in range(2):
        own[h] = fo_ref[:, h * half : (h + 1) * half] - mix(3, h)
    for h in range(2):
        cc[h].wait()
        cb[h].wait()
        lanes = slice(h * half, (h + 1) * half)
        res = own[h] - (c_in[h].astype(F32) + b_in[h].astype(F32))
        res_ref[:, lanes] = res
        rb = res.astype(BF)
        for g in range(2):
            q = 2 * h + g
            up = nt(rb[:, g * bsz : (g + 1) * bsz], inv_ref[q])
            at = slice(q * bsz, (q + 1) * bsz)
            upd_ref[:, at] = it_ref[:, at] + RELAXATION * up


def body(iterate, forcing, tiles, inverse_blocks, columns, coupling):
    modes, loads, dofs = iterate.shape
    terms, blocks, slots = tiles.shape[:3]
    bsz = dofs // blocks
    rows = modes * loads
    half = 2 * bsz
    seg = -(-rows // 128) * 128
    shaped = jnp.swapaxes(tiles.reshape(terms, blocks, slots, bsz, bsz), 1, 2)
    inverse = inverse_blocks.reshape(blocks, bsz, bsz)
    out = jax.ShapeDtypeStruct((rows, dofs), F32)
    sem2 = pltpu.SemaphoreType.DMA((2,))
    wire = pltpu.VMEM((2, rows, half), BF)
    vm = pl.BlockSpec(memory_space=pltpu.VMEM)
    flops = 2 * rows * (terms * slots * blocks * bsz * bsz + 4 * terms * seg * dofs)
    upd, res = pl.pallas_call(
        functools.partial(kernel, (modes, loads, bsz, terms, seg)),
        out_shape=(out, out),
        in_specs=[pl.BlockSpec(memory_space=pltpu.SMEM), vm, vm, ANY, ANY, ANY],
        out_specs=(vm, vm),
        scratch_shapes=[
            pltpu.VMEM((rows, dofs), F32),
            pltpu.VMEM((terms, slots, blocks, bsz, bsz), BF),
            pltpu.VMEM((blocks, bsz, bsz), BF),
            pltpu.VMEM((4, rows, half), BF),
            pltpu.VMEM((terms, blocks, rows, bsz), F32),
            pltpu.VMEM((2, terms * seg, half), BF),
            pltpu.VMEM((4, rows, terms * seg), BF),
            pltpu.VMEM((2, rows, half), F32),
            wire, wire, wire, wire, wire, wire,
            pltpu.SemaphoreType.DMA((3,)),
            sem2, sem2, sem2, sem2, sem2, sem2, sem2, sem2,
        ],
        compiler_params=pltpu.CompilerParams(
            collective_id=0, has_side_effects=True, vmem_limit_bytes=44 * 2**20
        ),
        cost_estimate=pl.CostEstimate(flops=flops, bytes_accessed=8 * 2**20, transcendentals=0),
    )(
        columns,
        iterate.reshape(rows, dofs),
        coupling,
        forcing.reshape(rows, dofs),
        shaped,
        inverse,
    )
    shape = (modes, loads, dofs)
    return upd.reshape(shape), res.reshape(shape)


def solution(mesh):
    return jax.shard_map(
        body,
        mesh=mesh,
        in_specs=(
            P("mode", None, "space"),
            P("mode", None, "space"),
            P(None, "space", None, None),
            P("space", None),
            P("space", None),
            P(),
        ),
        out_specs=(P("mode", None, "space"), P("mode", None, "space")),
        check_vma=False,
    )
```

time: 92.8 us -> 49.3 us (0.53)
  Pallas kernels: 0 us -> 34.6 us
  blocking collectives: 27.9 us -> 0 us
  waiting for transfers between devices: 24.5 us -> 0 us
  starting transfers between devices: 9.98 us -> 0 us
  matrix products: 6.89 us -> 0 us
  other arithmetic: 6.38 us -> 0 us
  local copies, waits for them, and re-layouts: 15.9 us -> 13.6 us
    pallas_call x0 -> x1, Pallas kernels: none -> 34.6 us  [body(): pl.pallas_call(functools.partial(kernel, (modes, loads, bsz, terms, seg))...]
    all_to_all x1 -> x0, blocking collectives: 27.9 us -> none  [body(): lax.all_to_all(products, 'mode', split_axis=3, concat_axis=1, tiled=True)]
    all_to_all x1 -> x0, waiting for transfers between devices: 17.3 us -> none  [body(): lax.all_to_all(mixture, 'mode', split_axis=0, concat_axis=2, tiled=True)]
    ppermute x2 -> x0, waiting for transfers between devices: 7.22 us -> none  [the longest x1 5.02 us: padded(): before = lax.ppermute(last, axis, up)]
    dot_general x3 -> x0, matrix products: 6.89 us -> none  [the longest x1 4.43 us: stiffness(): jnp.einsum('krsim,plrsm->kplri', shaped, picked, preferred_element_type=j...]
    unnamed x6 -> x12, local copies, waits for them, and re-layouts: 0.02 us -> 6.26 us
    ppermute x2 -> x0, starting transfers between devices: 6.12 us -> none  [the longest x1 3.1 us: padded(): after = lax.ppermute(initial, axis, down)]
    all_to_all x1 -> x0, starting transfers between devices: 3.86 us -> none  [body(): lax.all_to_all(mixture, 'mode', split_axis=0, concat_axis=2, tiled=True)]
  transfers between devices with their start and end apart: 3 -> 0, of which waited for: 3 -> 0; matrix products, arithmetic and copies ran while one was open for 8% -> 0% of each run, Pallas kernels for 0% -> 0%
where the time goes in v1:
time: 49.3 us; the launch traced here: 48.9 us
  Pallas kernels  34.6 us (70%)
  local copies, waits for them, and re-layouts  13.6 us (28%)
  between operations  0.67 us (1%)
    pallas_call x1, Pallas kernels, body(): pl.pallas_call(functools.partial(kernel, (modes, loads, bsz, terms, seg))...  34.6 us
    unnamed x12, local copies, waits for them, and re-layouts  6.26 us
    reshape x1, local copies, waits for them, and re-layouts, body(): shaped = jnp.swapaxes(tiles.reshape(terms, blocks, slots, bsz, bsz), 1, 2)  5.22 us
    reshape x1, local copies, waits for them, and re-layouts, body(): inverse = inverse_blocks.reshape(blocks, bsz, bsz)  2.15 us

profile of v1, /device:TPU:0, one launch (start us, length us, event | category | flops | bytes accessed | tf_op | source)
XLA Modules:
  0.0 48.9 jit_solution(11417329964197854527)
XLA Ops:
  0.6 0.0 copy-start.4
  0.6 2.1 %reshape.25.inv_hbm = bf16[4,192,192]{2,1,0:T(8,128)(2,1)} reshape(bf16[4,36864]{1,0:T(4,128)(2,1)} %param.9) | data formatting | bytes 589824 | tf_op jit(solution)/shard_map/reshape | solution.py:167
  2.8 5.2 %reshape.24 = bf16[3,4,3,192,192]{4,3,1,2,0:T(8,128)(2,1)S(1)} reshape(bf16[3,4,3,36864]{3,1,2,0:T(4,128)(2,1)} %param.8) | data formatting | bytes 5308416 | tf_op jit(solution)/shard_map/reshape | solution.py:166
  8.0 0.0 copy-done.4
  8.0 0.0 copy-start
  8.0 1.0 %copy-done = bf16[4,192,192]{2,1,0:T(8,128)(2,1)S(1)} copy-done((bf16[4,192,192]{2,1,0:T(8,128)(2,1)S(1)}, bf16[4,192,192]{2,1,0:T(8,128)(2,1)}, u32[]{:S(2)}) %copy-start) | copy-done | bytes 294936
  9.0 0.0 copy-start.1
  9.0 1.2 %copy-done.1 = f32[21,16,768]{2,1,0:T(8,128)S(1)} copy-done((f32[21,16,768]{2,1,0:T(8,128)S(1)}, f32[21,16,768]{2,1,0:T(8,128)}, u32[]{:S(2)}) %copy-start.1) | copy-done | bytes 1032216
  10.2 0.0 copy-start.2
  10.2 1.2 %copy-done.2 = f32[21,16,768]{2,1,0:T(8,128)S(1)} copy-done((f32[21,16,768]{2,1,0:T(8,128)S(1)}, f32[21,16,768]{2,1,0:T(8,128)}, u32[]{:S(2)}) %copy-start.2) | copy-done | bytes 1032216
  11.5 0.0 copy-start.3
  11.5 0.9 %copy-done.3 = f32[3,84,84]{2,1,0:T(8,128)S(1)} copy-done((f32[3,84,84]{2,1,0:T(8,128)S(1)}, f32[3,84,84]{2,1,0:T(8,128)}, u32[]{:S(2)}) %copy-start.3) | copy-done | bytes 84696
  12.4 34.6 %shard_map.77 = (f32[336,768]{1,0:T(8,128)S(1)}, f32[336,768]{1,0:T(8,128)S(1)}) custom-call(s32[4,3]{1,0:T(4,128)S(1)} %copy-done.4, f32[336,768]{1,0:T(8,128)S(1)} %bitcast.10, f32[3,84,84]{2,1,0:T(8,128)S(1)} %copy-done.3, f32[336,768]{1,0:T(8,128)S(1)} %bitcast.11, bf16[3,3,4,192,192]{4,3,2,1,0:T(8,128)(2,1)S(1)} %bitcast.7, bf16[4,192,192]{2,1,0:T(8,128)(2,1)S(1)} %copy-done), custom_call_target="tpu_custom_call" | custom-call | flops 3269984256 | bytes 8388608 | tf_op jit(solution)/shard_map/pallas_call | solution.py:173
  47.0 1.0 %copy.10 = f32[21,16,768]{2,1,0:T(8,128)} copy(f32[21,16,768]{2,1,0:T(8,128)S(1)} %bitcast.9) | data formatting | bytes 2064384
  48.0 1.0 %copy.11 = f32[21,16,768]{2,1,0:T(8,128)} copy(f32[21,16,768]{2,1,0:T(8,128)S(1)} %bitcast.8) | data formatting | bytes 2064384
Async XLA Ops:
  0.6 7.4 %copy-start.4 = (s32[4,3]{1,0:T(4,128)S(1)}, s32[4,3]{1,0:T(4,128)}, u32[]{:S(2)}) copy-start(s32[4,3]{1,0:T(4,128)} %cols_ref.1) | copy-start | bytes 148
  8.0 1.0 %copy-start = (bf16[4,192,192]{2,1,0:T(8,128)(2,1)S(1)}, bf16[4,192,192]{2,1,0:T(8,128)(2,1)}, u32[]{:S(2)}) copy-start(bf16[4,192,192]{2,1,0:T(8,128)(2,1)} %reshape.25.inv_hbm) | copy-start | bytes 884740
  9.0 1.2 %copy-start.1 = (f32[21,16,768]{2,1,0:T(8,128)S(1)}, f32[21,16,768]{2,1,0:T(8,128)}, u32[]{:S(2)}) copy-start(f32[21,16,768]{2,1,0:T(8,128)} %param.6) | copy-start | bytes 3096580
  10.2 1.2 %copy-start.2 = (f32[21,16,768]{2,1,0:T(8,128)S(1)}, f32[21,16,768]{2,1,0:T(8,128)}, u32[]{:S(2)}) copy-start(f32[21,16,768]{2,1,0:T(8,128)} %param.7) | copy-start | bytes 3096580
  11.5 0.9 %copy-start.3 = (f32[3,84,84]{2,1,0:T(8,128)S(1)}, f32[3,84,84]{2,1,0:T(8,128)}, u32[]{:S(2)}) copy-start(f32[3,84,84]{2,1,0:T(8,128)} %c_ref.1) | copy-start | bytes 254020

commit v2 on v1

--- a/solution.py
+++ b/solution.py
@@ -11,7 +11,7 @@
 BF = jnp.bfloat16
 F32 = jnp.float32
 MESH = pl.DeviceIdType.MESH
-ANY = pl.BlockSpec(memory_space=pl.ANY)
+HBM = pl.BlockSpec(memory_space=pltpu.HBM)
 
 
 def nt(a, b):
@@ -26,12 +26,33 @@
     return lax.broadcasted_iota(jnp.int32, shape, dim)
 
 
+def unpack(raw, dst, flat, tall, blocks, bsz):
+    pairs = bsz // 2
+    for t in range(bsz * bsz // 512):
+        v = raw[:, t * 512 : (t + 1) * 512].astype(F32)
+        for u in range(4):
+            at = (4 * t + u) * blocks
+            flat[at : at + blocks, :] = v[:, u * 128 : (u + 1) * 128]
+    for j in range(blocks):
+        a, b, c = [flat[pl.ds(n * blocks + j, pairs, 3 * blocks), :] for n in range(3)]
+        turned = pltpu.roll(b, 64, 1)
+        low = iota((pairs, 128), 1) < 64
+        rolled = pltpu.roll(c, 64, 1)
+        tall[0, pl.ds(0, pairs, 2), :] = a
+        tall[1, pl.ds(0, pairs, 2), :] = b
+        tall[0, pl.ds(1, pairs, 2), :] = jnp.where(low, turned, rolled)
+        tall[1, pl.ds(1, pairs, 2), :] = rolled
+        dst[j, :, 0:128] = tall[0].astype(BF)
+        dst[j, :, 128:bsz] = tall[1][:, : bsz - 128].astype(BF)
+
+
 def kernel(
     cfg,
-    cols_ref, it_ref, c_ref, fo_hbm, tiles_hbm, inv_hbm,
+    cols_ref, it_hbm, c_hbm, fo_hbm, tiles_hbm, inv_hbm,
     upd_ref, res_ref,
-    fo_ref, tiles_ref, inv_ref, xe, acc, prod, kron, own, a_out, a_in, b_out, b_in, c_out, c_in,
-    lsem, hs, hr, as_, ar, bs, br, cs, cr,
+    it_ref, c_ref, fo_ref, tiles_ref, inv_ref, xe, acc, prod, kron, own, a_out, a_in, b_out, b_in, c_out, c_in,
+    raw_ref, raw_inv, flat, tall,
+    isem, lsem, hs, hr, as_, ar, bs, br, cs, cr,
 ):
     modes, loads, bsz, terms, seg = cfg
     rows = modes * loads
@@ -47,18 +68,29 @@
     to_right, to_left = (right, me), (left, me)
     to_near, to_far = (me_s, near), (me_s, far)
 
+    barrier = pltpu.get_barrier_semaphore()
+    for who in (to_right, to_left, to_near, to_far):
+        pl.semaphore_signal(barrier, inc=1, device_id=who, device_id_type=MESH)
+    it_in = [
+        pltpu.make_async_copy(
+            it_hbm.at[:, pl.ds(h * half, half)], it_ref.at[:, pl.ds(h * half, half)], isem.at[h]
+        )
+        for h in range(2)
+    ]
+    c_in_ = pltpu.make_async_copy(c_hbm, c_ref, isem.at[2])
+    for cp in it_in:
+        cp.start()
+    c_in_.start()
     loads_in = [
-        pltpu.make_async_copy(tiles_hbm, tiles_ref, lsem.at[0]),
+        pltpu.make_async_copy(tiles_hbm, raw_ref, lsem.at[0]),
         pltpu.make_async_copy(fo_hbm, fo_ref, lsem.at[1]),
-        pltpu.make_async_copy(inv_hbm, inv_ref, lsem.at[2]),
+        pltpu.make_async_copy(inv_hbm, raw_inv, lsem.at[2]),
     ]
     for cp in loads_in:
         cp.start()
 
-    barrier = pltpu.get_barrier_semaphore()
-    for who in (to_right, to_left, to_near, to_far):
-        pl.semaphore_signal(barrier, inc=1, device_id=who, device_id_type=MESH)
-    for h in range(2):
+    for h in range(2):
+        it_in[h].wait()
         xe[1 + h] = it_ref[:, h * half : (h + 1) * half].astype(BF)
     pl.semaphore_wait(barrier, 4)
 
@@ -74,6 +106,7 @@
     for cp in halo:
         cp.start()
 
+    c_in_.wait()
     total = c_ref.shape[1]
     col = iota((total, seg), 1)
     pick = (iota((total, seg), 0) == me * modes + col // loads) & (col < rows)
@@ -94,6 +127,10 @@
         return xe[p // 2, :, (p % 2) * bsz : (p % 2 + 1) * bsz]
 
     loads_in[0].wait()
+
+    @pl.loop(0, terms * 3)
+    def _(n):
+        unpack(raw_ref.at[n // 3, n % 3], tiles_ref.at[n // 3, n % 3], flat, tall, 4, bsz)
 
     def early(q, s):
         near_, far_ = (q - 1, q - 2) if s == 1 else (q + 1, q + 2)
@@ -131,6 +168,7 @@
         late(h)
         a_out[h] = mix(0, h).astype(BF)
         ca[h].start()
+    for h in range(2):
         t = mix(1, h)
         ca[h].wait()
         b_out[h] = (t + a_in[h].astype(F32)).astype(BF)
@@ -140,6 +178,7 @@
         cc[h].start()
     loads_in[1].wait()
     loads_in[2].wait()
+    unpack(raw_inv, inv_ref, flat, tall, 4, bsz)
     for h in range(2):
         own[h] = fo_ref[:, h * half : (h + 1) * half] - mix(3, h)
     for h in range(2):
@@ -163,8 +202,7 @@
     rows = modes * loads
     half = 2 * bsz
     seg = -(-rows // 128) * 128
-    shaped = jnp.swapaxes(tiles.reshape(terms, blocks, slots, bsz, bsz), 1, 2)
-    inverse = inverse_blocks.reshape(blocks, bsz, bsz)
+    shaped = jnp.swapaxes(tiles, 1, 2)
     out = jax.ShapeDtypeStruct((rows, dofs), F32)
     sem2 = pltpu.SemaphoreType.DMA((2,))
     wire = pltpu.VMEM((2, rows, half), BF)
@@ -173,9 +211,11 @@
     upd, res = pl.pallas_call(
         functools.partial(kernel, (modes, loads, bsz, terms, seg)),
         out_shape=(out, out),
-        in_specs=[pl.BlockSpec(memory_space=pltpu.SMEM), vm, vm, ANY, ANY, ANY],
+        in_specs=[pl.BlockSpec(memory_space=pltpu.SMEM), HBM, HBM, HBM, HBM, HBM],
         out_specs=(vm, vm),
         scratch_shapes=[
+            pltpu.VMEM((rows, dofs), F32),
+            pltpu.VMEM(coupling.shape, F32),
             pltpu.VMEM((rows, dofs), F32),
             pltpu.VMEM((terms, slots, blocks, bsz, bsz), BF),
             pltpu.VMEM((blocks, bsz, bsz), BF),
@@ -185,6 +225,11 @@
             pltpu.VMEM((4, rows, terms * seg), BF),
             pltpu.VMEM((2, rows, half), F32),
             wire, wire, wire, wire, wire, wire,
+            pltpu.VMEM(tuple(tiles.shape[i] for i in (0, 2, 1, 3)), BF),
+            pltpu.VMEM(inverse_blocks.shape, BF),
+            pltpu.VMEM((blocks * bsz * bsz // 128, 128), F32),
+            pltpu.VMEM((2, bsz, 128), F32),
+            pltpu.SemaphoreType.DMA((3,)),
             pltpu.SemaphoreType.DMA((3,)),
             sem2, sem2, sem2, sem2, sem2, sem2, sem2, sem2,
         ],
@@ -198,7 +243,7 @@
         coupling,
         forcing.reshape(rows, dofs),
         shaped,
-        inverse,
+        inverse_blocks,
     )
     shape = (modes, loads, dofs)
     return upd.reshape(shape), res.reshape(shape)

time: 49.3 us -> 43.3 us (0.88)
  local copies, waits for them, and re-layouts: 13.6 us -> 8.65 us
  Pallas kernels: 34.6 us -> 33.7 us
    reshape x2 -> x0, local copies, waits for them, and re-layouts: 7.36 us -> none  [the longest x1 5.22 us: body(): shaped = jnp.swapaxes(tiles.reshape(terms, blocks, slots, bsz, bsz), 1, 2)]
    unnamed x12 -> x14, local copies, waits for them, and re-layouts: 6.26 us -> 8.65 us
    pallas_call x1, Pallas kernels: 34.6 us -> 33.7 us  [body(): pl.pallas_call(functools.partial(kernel, (modes, loads, bsz, terms, seg))...]
where the time goes in v2:
time: 43.3 us; the launch traced here: 43 us
  Pallas kernels  33.7 us (78%)
  local copies, waits for them, and re-layouts  8.65 us (20%)
  between operations  0.65 us (2%)
    pallas_call x1, Pallas kernels, body(): pl.pallas_call(functools.partial(kernel, (modes, loads, bsz, terms, seg))...  33.7 us
    unnamed x14, local copies, waits for them, and re-layouts  8.65 us

profile of v2, /device:TPU:0, one launch (start us, length us, event | category | flops | bytes accessed | tf_op | source)
XLA Modules:
  0.0 43.0 jit_solution(8099429769069024762)
XLA Ops:
  0.6 0.0 copy-start
  0.6 1.7 %copy-done = bf16[3,4,3,36864]{3,1,2,0:T(4,128)(2,1)S(1)} copy-done((bf16[3,4,3,36864]{3,1,2,0:T(4,128)(2,1)S(1)}, bf16[3,4,3,36864]{3,1,2,0:T(4,128)(2,1)}, u32[]{:S(2)}) %copy-start) | copy-done | bytes 2654232
  2.4 0.0 copy-start.1
  2.4 1.2 %copy-done.1 = f32[21,16,768]{2,1,0:T(8,128)S(1)} copy-done((f32[21,16,768]{2,1,0:T(8,128)S(1)}, f32[21,16,768]{2,1,0:T(8,128)}, u32[]{:S(2)}) %copy-start.1) | copy-done | bytes 1032216
  3.6 0.0 copy-start.2
  3.6 1.2 %copy-done.2 = f32[21,16,768]{2,1,0:T(8,128)S(1)} copy-done((f32[21,16,768]{2,1,0:T(8,128)S(1)}, f32[21,16,768]{2,1,0:T(8,128)}, u32[]{:S(2)}) %copy-start.2) | copy-done | bytes 1032216
  4.8 0.0 copy-start.3
  4.8 1.0 %copy-done.3 = bf16[4,36864]{1,0:T(4,128)(2,1)S(1)} copy-done((bf16[4,36864]{1,0:T(4,128)(2,1)S(1)}, bf16[4,36864]{1,0:T(4,128)(2,1)}, u32[]{:S(2)}) %copy-start.3) | copy-done | bytes 294936
  5.8 0.0 copy-start.4
  5.8 0.9 %copy-done.4 = f32[3,84,84]{2,1,0:T(8,128)S(1)} copy-done((f32[3,84,84]{2,1,0:T(8,128)S(1)}, f32[3,84,84]{2,1,0:T(8,128)}, u32[]{:S(2)}) %copy-start.4) | copy-done | bytes 84696
  6.7 0.0 copy-start.5
  6.7 0.7 %copy-done.5 = s32[4,3]{1,0:T(4,128)S(1)} copy-done((s32[4,3]{1,0:T(4,128)S(1)}, s32[4,3]{1,0:T(4,128)}, u32[]{:S(2)}) %copy-start.5) | copy-done | bytes 72
  7.4 33.7 %shard_map.77 = (f32[336,768]{1,0:T(8,128)S(1)}, f32[336,768]{1,0:T(8,128)S(1)}) custom-call(s32[4,3]{1,0:T(4,128)S(1)} %copy-done.5, f32[336,768]{1,0:T(8,128)S(1)} %bitcast.8, f32[3,84,84]{2,1,0:T(8,128)S(1)} %copy-done.4, f32[336,768]{1,0:T(8,128)S(1)} %bitcast.9, bf16[3,3,4,36864]{3,2,1,0:T(4,128)(2,1)S(1)} %bitcast.7, bf16[4,36864]{1,0:T(4,128)(2,1)S(1)} %copy-done.3), custom_call_target="tpu_custom_call" | custom-call | flops 3269984256 | bytes 8388608 | tf_op jit(solution)/shard_map/pallas_call | solution.py:211
  41.1 1.0 %copy.10 = f32[21,16,768]{2,1,0:T(8,128)} copy(f32[21,16,768]{2,1,0:T(8,128)S(1)} %bitcast.6) | data formatting | bytes 2064384
  42.0 1.0 %copy.11 = f32[21,16,768]{2,1,0:T(8,128)} copy(f32[21,16,768]{2,1,0:T(8,128)S(1)} %bitcast.5) | data formatting | bytes 2064384
Async XLA Ops:
  0.6 1.8 %copy-start = (bf16[3,4,3,36864]{3,1,2,0:T(4,128)(2,1)S(1)}, bf16[3,4,3,36864]{3,1,2,0:T(4,128)(2,1)}, u32[]{:S(2)}) copy-start(bf16[3,4,3,36864]{3,1,2,0:T(4,128)(2,1)} %param.8) | copy-start | bytes 7962628
  2.4 1.2 %copy-start.1 = (f32[21,16,768]{2,1,0:T(8,128)S(1)}, f32[21,16,768]{2,1,0:T(8,128)}, u32[]{:S(2)}) copy-start(f32[21,16,768]{2,1,0:T(8,128)} %param.6) | copy-start | bytes 3096580
  3.6 1.2 %copy-start.2 = (f32[21,16,768]{2,1,0:T(8,128)S(1)}, f32[21,16,768]{2,1,0:T(8,128)}, u32[]{:S(2)}) copy-start(f32[21,16,768]{2,1,0:T(8,128)} %param.7) | copy-start | bytes 3096580
  4.8 1.0 %copy-start.3 = (bf16[4,36864]{1,0:T(4,128)(2,1)S(1)}, bf16[4,36864]{1,0:T(4,128)(2,1)}, u32[]{:S(2)}) copy-start(bf16[4,36864]{1,0:T(4,128)(2,1)} %inv_hbm.1) | copy-start | bytes 884740
  5.8 0.9 %copy-start.4 = (f32[3,84,84]{2,1,0:T(8,128)S(1)}, f32[3,84,84]{2,1,0:T(8,128)}, u32[]{:S(2)}) copy-start(f32[3,84,84]{2,1,0:T(8,128)} %c_hbm.1) | copy-start | bytes 254020
  6.7 0.7 %copy-start.5 = (s32[4,3]{1,0:T(4,128)S(1)}, s32[4,3]{1,0:T(4,128)}, u32[]{:S(2)}) copy-start(s32[4,3]{1,0:T(4,128)} %cols_ref.1) | copy-start | bytes 148
